TPU v7x, 32 devices: a whole 2x2x4 slice. The times are simulated.
32 devices in a mesh: wave: 32 (over z, y, x, core), lev: 1.
Axes of the slice: x: 2, y: 2, z: 4, core: 2. Of those that a mesh axis runs over, the one named last changes fastest.
Arguments:
- spectra: bfloat16 [640, 16, 2, 640], P('wave', 'lev'), may hold values from -0.3125 to 0.3125
- legendre: bfloat16 [640, 32, 640], P('wave'), may hold values from -0.25 to 0.25
- wave_slots: int32 [640], replicated, may hold values from 0 to 639, each once
- row_cycle: int32 [32], replicated, may hold values from 0 to 1279, as said below
Outputs:
- grid_fields: bfloat16 [16, 32, 6144], P(None, 'wave', 'lev')
Inputs may be any that keep to these rules, and one draw needn't show every extreme that they name: `wave_slots`: each wavenumber 0 to 639 stands in exactly one slot; slot r lies on wave index r // 20. `row_cycle`: cycle numbers of distinct rows differ; cycle 0 and cycle 1280 - 1 both occur; row q lies on wave index q.
All inputs are finite; a program needn't handle non-finite values.
Results may differ from a plain program's by a relative error of at most 0.0055.
Values may be sent and summed in bfloat16 or wider, within the bound.
A program may use at most 64 MiB of HBM per device.

v0:
```python
from functools import partial
import math

import jax
import jax.numpy as jnp
from jax import lax
from jax.sharding import PartitionSpec as P

NLON = 6144


two_pi = 2.0 * math.pi


def twiddle_table(slot_waves, row_points, first_col, col_count):
    columns = first_col + lax.iota(jnp.int32, col_count)
    phase_int = slot_waves[:, None] * columns[None, :] % row_points
    angles = jnp.float32(two_pi) * phase_int.astype(jnp.float32) / row_points.astype(jnp.float32)
    weight = jnp.where(slot_waves == 0, jnp.float32(1.0), jnp.float32(2.0))[:, None]
    inside = (columns < row_points)[None, :]
    cosine = jnp.where(inside, weight * jnp.cos(angles), jnp.float32(0.0))
    sine_part = jnp.where(inside, -weight * jnp.sin(angles), jnp.float32(0.0))
    return jnp.concatenate([cosine, sine_part], axis=0).astype(jnp.bfloat16)


def row_product(coeffs, twiddle):
    return jnp.dot(coeffs, twiddle, preferred_element_type=jnp.float32).astype(jnp.bfloat16)


def shards(spectra, legendre, wave_slots, row_cycle):
    slots_dev, pairs_dev, two_parts, degrees = spectra.shape
    wave_count = lax.axis_size("wave")
    level_count = lax.axis_size("lev")
    total_slots = slots_dev * wave_count
    wave_pos = lax.axis_index("wave")
    level_pos = lax.axis_index("lev")
    own_waves = lax.dynamic_slice_in_dim(wave_slots, wave_pos * slots_dev, slots_dev)
    degree = lax.iota(jnp.int32, degrees)
    keep_mask = degree[None, :] < (total_slots - own_waves)[:, None]
    masked = jnp.where(keep_mask[:, None, None, :], spectra, jnp.zeros((), spectra.dtype))
    fourier = jnp.einsum(
        "rpik,rlk->plir", masked, legendre, preferred_element_type=jnp.float32
    ).astype(jnp.bfloat16)
    by_rows = lax.all_to_all(fourier, "wave", split_axis=1, concat_axis=3, tiled=True)
    rows_dev = by_rows.shape[1]
    flat_width = 2 * total_slots
    own_cycles = lax.dynamic_slice_in_dim(row_cycle, wave_pos * rows_dev, rows_dev)
    region = NLON // level_count
    first_col = level_pos * region
    actives = []
    row_pos = 0
    row_points = 20 + 4 * own_cycles[row_pos]
    active = first_col < row_points
    twiddle = twiddle_table(wave_slots, row_points, first_col, region)
    tables = [twiddle]
    actives.append(active)
    piece = lax.all_gather(by_rows, "lev", axis=0, tiled=True)
    row_pos = 0
    coeffs = piece[:, row_pos].reshape(piece.shape[0], flat_width)
    product = partial(row_product, coeffs, tables[row_pos])
    results = [product()]
    return jnp.stack(results, axis=1)


def solution(mesh):
    placed = (P("wave", "lev", None, None), P("wave", None, None), P(), P())
    return jax.shard_map(
        shards, mesh=mesh, in_specs=placed, out_specs=P(None, "wave", "lev"), check_vma=False
    )
```

profile of v0, /device:TPU:0, one launch (start us, length us, event | category | flops | bytes accessed | tf_op | source)
XLA Modules:
  0.0 236.1 jit_solution(6809609361605725039)
XLA Ops:
  0.0 0.0 copy-start
  0.0 0.8 dynamic-slice_subtract_fusion
  0.8 0.1 iota_compare_fusion
  0.9 1.9 broadcast_select_fusion
  2.8 0.0 copy-done
  2.8 0.4 fusion.17
  3.2 0.6 copy.12
  3.7 1.0 reshape.32
  4.7 7.3 %all-to-all-start = ((bf16[32,2,320]{2,1,0:T(2,128)(2,1)}), bf16[32,2,320]{2,1,0:T(2,128)(2,1)S(1)}, u32[]{:S(2)}, u32[]{:S(2)}) async-start(bf16[32,2,320]{2,1,0:T(2,128)(2,1)} %reshape.32), calls=%async_computation | async-start | bytes 98304 | tf_op jit(solution)/shard_map/all_to_all | solution.py:44
  12.0 1.3 dynamic_slice.7
  13.9 0.7 compare_select_fusion
  14.6 213.3 %select_convert_fusion.1 = (bf16[640,6144]{1,0:T(8,128)(2,1)}, bf16[640,6144]{1,0:T(8,128)(2,1)}) fusion(f32[640]{0:T(1024)S(1)} %get-tuple-element.7, f32[]{:T(128)S(6)} %convert_element_type.19, pred[]{:T(512)S(6)} %lt.49, s32[]{:T(128)S(6)} %select_n.34, s32[640]{0:T(1024)} %param.6, pred[6144]{0:T(1024)(128)(4,1)S(1)} %iota_compare_fusion.1, ...), kind=kLoop, calls=%fused_computation.9 | loop fusion | flops 66846720 | bytes 15742473 | tf_op jit(solution)/shard_map/convert
  227.9 0.0 all-to-all-done
  227.9 0.4 reshape.33
  228.3 0.1 copy.13
  228.4 0.3 reshape_squeeze.3
  228.8 7.4 %fusion.14 = bf16[16,1,6144]{2,0,1:T(8,128)(2,1)} fusion(bf16[16,1280]{1,0:T(8,128)(2,1)S(1)} %reshape_squeeze.3, bf16[640,6144]{1,0:T(8,128)(2,1)} %get-tuple-element.6, bf16[640,6144]{1,0:T(8,128)(2,1)} %get-tuple-element.5), kind=kOutput, calls=%fused_computation.16 | convolution fusion | flops 283213824 | bytes 15966208 | tf_op jit(solution)/shard_map/dot_general | solution.py:27
  (2 shorter events, 0.0 us)
Async XLA Ops:
  0.0 2.8 %copy-start = (bf16[20,32,640]{2,1,0:T(8,128)(2,1)S(1)}, bf16[20,32,640]{2,1,0:T(8,128)(2,1)}, u32[]{:S(2)}) copy-start(bf16[20,32,640]{2,1,0:T(8,128)(2,1)} %param.5) | copy-start | bytes 2457604
  4.7 223.2 %all-to-all-start = ((bf16[32,2,320]{2,1,0:T(2,128)(2,1)}), bf16[32,2,320]{2,1,0:T(2,128)(2,1)S(1)}, u32[]{:S(2)}, u32[]{:S(2)}) async-start(bf16[32,2,320]{2,1,0:T(2,128)(2,1)} %reshape.32), calls=%async_computation | async-start | bytes 98304 | tf_op jit(solution)/shard_map/all_to_all | solution.py:44
where the time goes:
time: 236 us
  other arithmetic  217 us (92%)
  matrix products  7.76 us (3%)
  starting transfers between devices  7.3 us (3%)
  local copies, waits for them, and re-layouts  3.6 us (2%)
    another operation x1, other arithmetic  213 us
    dot_general x1, matrix products, row_product(): jnp.dot(coeffs, twiddle, preferred_element_type=jnp.float32)  7.38 us
    all_to_all x1, starting transfers between devices, shards(): lax.all_to_all(fourier, 'wave', split_axis=1, concat_axis=3, tiled=True)  7.3 us
  transfers between devices with their start and end apart: 1, of which 0 were waited for; matrix products, arithmetic and copies ran while one was open for 91% of the time, Pallas kernels for 0%

commit v1 on v0

v1 whole, which is shorter than its diff:
```python
import functools
import math

import jax
import jax.numpy as jnp
from jax import lax
from jax.experimental import pallas as pl
from jax.experimental.pallas import tpu as pltpu
from jax.sharding import PartitionSpec as P

NLON = 6144
CYCLES = 1280
BLOCK = 256
FINE = 16
NT = (((1,), (1,)), ((), ()))


def iota(shape, axis):
    return lax.broadcasted_iota(jnp.int32, shape, axis)


def sincos(waves, steps, points, inverse):
    product = waves * steps
    rest = product - jnp.round(product * inverse) * points
    half = rest * inverse * jnp.float32(math.pi)
    square = half * half
    sine = jnp.full_like(square, 1.0 / math.factorial(13))
    cosine = jnp.full_like(square, 1.0 / math.factorial(12))
    for order in (11, 9, 7, 5, 3, 1):
        sign = -1.0 if order % 4 == 3 else 1.0
        sine = sine * square + jnp.float32(sign / math.factorial(order))
        sign = -1.0 if (order - 1) % 4 == 2 else 1.0
        cosine = cosine * square + jnp.float32(sign / math.factorial(order - 1))
    sine = sine * half
    return 1.0 - 2.0 * sine * sine, 2.0 * sine * cosine


def kernel(
    waves, levs, blocks,
    slots_smem, cycle_smem, slots_ref, spectra_ref, legendre_ref, out_ref,
    spec, leg, send, recv, inner, in_sem, send_sem, recv_sem,
):
    slots_dev, pairs_dev, _, degrees = spectra_ref.shape
    rows = legendre_ref.shape[1]
    total = slots_dev * waves
    lanes = 2 * pairs_dev
    group = 128 // lanes
    groups = slots_dev // group
    devices = waves * levs
    me = lax.axis_index("wave")
    lev = lax.axis_index("lev")
    here = me * levs + lev

    def peer(step):
        there = lax.rem(here + step, devices)
        return lax.div(there, levs), lax.rem(there, levs)

    barrier = pltpu.get_barrier_semaphore()

    def greet(step, carry):
        wave_to, lev_to = peer(step)
        pl.semaphore_signal(
            barrier, inc=1, device_id={"wave": wave_to, "lev": lev_to},
            device_id_type=pl.DeviceIdType.MESH,
        )
        return carry

    loads = []
    for g in range(groups):
        part = pl.ds(g * group, group)
        loads.append((
            pltpu.make_async_copy(spectra_ref.at[part], spec.at[part], in_sem.at[0, g]),
            pltpu.make_async_copy(legendre_ref.at[part], leg.at[part], in_sem.at[1, g]),
        ))
    for pair in loads:
        for copy in pair:
            copy.start()
    lax.fori_loop(1, devices, greet, 0)

    points_int = 20 + 4 * cycle_smem[me]
    points = points_int.astype(jnp.float32)
    slots = slots_ref[...]
    slot_rows = 32
    within = iota((slot_rows, total), 1).astype(jnp.float32)
    owner = jnp.floor((within + 0.5) * jnp.float32(1.0 / slots_dev))
    is_slot = within - owner * slots_dev == iota((slot_rows, total), 0).astype(jnp.float32)
    wide = group * waves
    column = iota((wide, total), 1).astype(jnp.float32)
    column_owner = jnp.floor((column + 0.5) * jnp.float32(1.0 / slots_dev))
    wave_row = lax.rem(iota((wide, 1), 0), waves).astype(jnp.float32)
    is_owner = jnp.where(column_owner == wave_row, 1.0, 0.0).astype(jnp.bfloat16)
    ordered = jnp.zeros((slot_rows, wide), jnp.float32)
    for part, scale in ((jnp.right_shift(slots, 7), 128.0), (jnp.bitwise_and(slots, 127), 1.0)):
        chosen = jnp.where(is_slot, part.astype(jnp.float32), 0.0).astype(jnp.bfloat16)
        ordered += scale * lax.dot_general(
            chosen, is_owner, NT, preferred_element_type=jnp.float32
        )
    place = lax.div(iota((1, wide), 1), waves)
    pieces = []
    for g in range(groups):
        piece = jnp.zeros((1, wide), jnp.float32)
        for k in range(group):
            row = g * group + k
            piece = jnp.where(place == k, ordered[row : row + 1], piece)
        pieces.append(piece)
    order_waves = jnp.concatenate(pieces, axis=1)
    inverse = 1.0 / jnp.full((1, 1), points, jnp.float32)

    def table(count, stride, first):
        steps = (iota((count, total), 0) * stride + first).astype(jnp.float32)
        return sincos(order_waves, steps, points, inverse)

    degree = iota((1, degrees), 1)
    lane_slot = lax.div(iota((rows, 128), 1), lanes)
    for g in range(groups):
        for copy in loads[g]:
            copy.wait()
        kept = []
        for k in range(group):
            r = g * group + k
            limit = total - slots_smem[me * slots_dev + r]
            keep = jnp.where(degree < limit, 1.0, 0.0).astype(jnp.bfloat16)
            kept.append(spec[r].reshape(lanes, degrees) * keep)
        values = leg[pl.ds(g * group, group)].reshape(group * rows, degrees)
        product = lax.dot_general(
            values, jnp.concatenate(kept, axis=0), NT, preferred_element_type=jnp.float32
        )
        fourier = product[:rows]
        for k in range(1, group):
            fourier = jnp.where(lane_slot == k, product[k * rows : (k + 1) * rows], fourier)
        fourier = fourier.astype(jnp.bfloat16).astype(jnp.float32)
        send[:, :, pl.ds(g * 128, 128)] = fourier.reshape(rows, 1, 128)

    slot_here = lev * waves + me
    pl.semaphore_wait(barrier, devices - 1)

    def deliver(step, carry):
        wave_to, lev_to = peer(step)
        pltpu.make_async_remote_copy(
            src_ref=send.at[wave_to], dst_ref=recv.at[slot_here],
            send_sem=send_sem, recv_sem=recv_sem,
            device_id={"wave": wave_to, "lev": lev_to}, device_id_type=pl.DeviceIdType.MESH,
        ).start()
        return carry

    lax.fori_loop(1, devices, deliver, 0)
    recv[slot_here] = send[me]

    first = lev * (NLON // levs)
    coarse_cos, coarse_sin = table(BLOCK // FINE, FINE, 0)
    fine_cos, fine_sin = table(FINE, 1, 0)
    for a in range(BLOCK // FINE):
        ca, sa = coarse_cos[a : a + 1], coarse_sin[a : a + 1]
        inner[a * FINE : (a + 1) * FINE, :total] = (ca * fine_cos - sa * fine_sin).astype(jnp.bfloat16)
        inner[a * FINE : (a + 1) * FINE, total:] = (-(sa * fine_cos + ca * fine_sin)).astype(jnp.bfloat16)
    outer_cos, outer_sin = table(-(-blocks // 8) * 8, BLOCK, first)
    weight = jnp.where(order_waves == 0.0, 1.0, 2.0)
    pick_row = iota((lanes, 128), 0)
    pick_pair = jnp.where(pick_row < pairs_dev, 2 * pick_row, 2 * (pick_row - pairs_dev) + 1)
    pick = jnp.where(lax.rem(iota((lanes, 128), 1), lanes) == pick_pair, 1.0, 0.0).astype(jnp.bfloat16)
    arrived_slot = lax.div(iota((waves, 128), 1), lanes)

    for sem in (recv_sem, send_sem):
        all_of_them = recv.at[pl.ds(0, devices - 1)]
        pltpu.make_async_copy(all_of_them, all_of_them, sem).wait()

    reals, imags = [], []
    for v in range(levs):
        parts = []
        for g in range(groups):
            block = recv[v * waves : (v + 1) * waves, :, pl.ds(g * 128, 128)].reshape(waves, 128)
            spread = jnp.concatenate(
                [jnp.where(arrived_slot == k, block, 0.0) for k in range(group)], axis=0
            ).astype(jnp.bfloat16)
            parts.append(lax.dot_general(pick, spread, NT, preferred_element_type=jnp.float32))
        coeffs = jnp.concatenate(parts, axis=1) * weight
        reals.append(coeffs[:pairs_dev])
        imags.append(coeffs[pairs_dev:])
    real = jnp.concatenate(reals, axis=0)
    imag = jnp.concatenate(imags, axis=0)
    pairs = real.shape[0]

    at = iota((pairs, BLOCK), 1) + first
    step = 7 if blocks % 7 == 0 else 2
    for start in range(0, blocks, step):
        turned = []
        for j in range(start, start + step):
            c, s = outer_cos[j : j + 1], outer_sin[j : j + 1]
            turned.append(jnp.concatenate(
                [(real * c - imag * s).astype(jnp.bfloat16), (real * s + imag * c).astype(jnp.bfloat16)],
                axis=1,
            ))
        result = lax.dot_general(
            jnp.concatenate(turned, axis=0), inner[...], NT, preferred_element_type=jnp.float32
        )
        for j in range(start, start + step):
            found = result[(j - start) * pairs : (j - start + 1) * pairs]
            found = jnp.where(at + j * BLOCK < points_int, found, 0.0)
            out_ref[:, j * BLOCK : (j + 1) * BLOCK] = found.astype(jnp.bfloat16)
    if blocks * BLOCK < out_ref.shape[1]:
        rest = out_ref.shape[1] - blocks * BLOCK
        out_ref[:, blocks * BLOCK :] = jnp.zeros((pairs, rest), jnp.bfloat16)


def shards(spectra, legendre, wave_slots, row_cycle):
    waves = lax.axis_size("wave")
    levs = lax.axis_size("lev")
    slots_dev, pairs_dev, _, degrees = spectra.shape
    rows = legendre.shape[1]
    total = slots_dev * waves
    region = NLON // levs
    blocks = min(region // BLOCK, -(-(20 + 4 * (CYCLES - 1)) // BLOCK))
    width = slots_dev * 2 * pairs_dev
    smem = pl.BlockSpec(memory_space=pltpu.SMEM)
    vmem = pl.BlockSpec(memory_space=pltpu.VMEM)
    hbm = pl.BlockSpec(memory_space=pl.ANY)
    grid = pl.pallas_call(
        functools.partial(kernel, waves, levs, blocks),
        out_shape=jax.ShapeDtypeStruct((pairs_dev * levs, region), jnp.bfloat16),
        in_specs=[smem, smem, vmem, hbm, hbm],
        out_specs=vmem,
        scratch_shapes=[
            pltpu.VMEM((slots_dev, pairs_dev, 2, degrees), jnp.bfloat16),
            pltpu.VMEM((slots_dev, rows, degrees), jnp.bfloat16),
            pltpu.VMEM((rows, 1, width), jnp.float32),
            pltpu.VMEM((levs * waves, 1, width), jnp.float32),
            pltpu.VMEM((BLOCK, 2 * total), jnp.bfloat16),
            pltpu.SemaphoreType.DMA((2, slots_dev * 2 * pairs_dev // 128)),
            pltpu.SemaphoreType.DMA,
            pltpu.SemaphoreType.DMA,
        ],
        compiler_params=pltpu.CompilerParams(
            collective_id=0, has_side_effects=True, vmem_limit_bytes=48 << 20
        ),
    )(wave_slots, row_cycle, wave_slots.reshape(1, total), spectra, legendre)
    return grid.reshape(grid.shape[0], 1, region)


def solution(mesh):
    placed = (P("wave", "lev", None, None), P("wave", None, None), P(), P())
    return jax.shard_map(
        shards, mesh=mesh, in_specs=placed, out_specs=P(None, "wave", "lev"), check_vma=False
    )
```

time: 236 us -> 18.1 us (0.08)
  other arithmetic: 217 us -> 0 us
  Pallas kernels: 0 us -> 14.1 us
  matrix products: 7.76 us -> 0 us
  starting transfers between devices: 7.3 us -> 0 us
    another operation x1 -> x0, other arithmetic: 213 us -> none
    pallas_call x0 -> x1, Pallas kernels: none -> 14.1 us  [shards(): pl.pallas_call(functools.partial(kernel, waves, levs, blocks), out_shape=...]
    dot_general x2 -> x0, matrix products: 7.76 us -> none  [the longest x1 7.38 us: row_product(): jnp.dot(coeffs, twiddle, preferred_element_type=jnp.float32)]
    all_to_all x1 -> x0, starting transfers between devices: 7.3 us -> none  [shards(): lax.all_to_all(fourier, 'wave', split_axis=1, concat_axis=3, tiled=True)]
    select_n x2 -> x0, other arithmetic: 2.55 us -> none  [the longest x1 1.86 us: shards(): jnp.where(keep_mask[:, None, None, :], spectra, jnp.zeros((), spectra.dty...]
  transfers between devices with their start and end apart: 1 -> 0, of which waited for: 0 -> 0; matrix products, arithmetic and copies ran while one was open for 91% -> 0% of each run, Pallas kernels for 0% -> 0%
where the time goes in v1:
time: 18.1 us; the launch traced here: 17.9 us
  Pallas kernels  14.1 us (78%)
  local copies, waits for them, and re-layouts  3.73 us (21%)
    pallas_call x1, Pallas kernels, shards(): pl.pallas_call(functools.partial(kernel, waves, levs, blocks), out_shape=...  14.1 us
    unnamed x9, local copies, waits for them, and re-layouts  2.97 us
    reshape x1, local copies, waits for them, and re-layouts, shards(): wave_slots.reshape(1, total)  0.76 us

profile of v1, /device:TPU:0, one launch (start us, length us, event | category | flops | bytes accessed | tf_op | source)
XLA Modules:
  0.0 17.9 jit_solution(12668630935169197116)
XLA Ops:
  0.0 0.0 copy-start.2
  0.0 0.0 copy-start.3
  0.0 0.8 %reshape.6.slots_ref = s32[1,640]{1,0:T(1,128)S(1)} reshape(s32[640]{0:T(1024)} %slots_smem.1) | data formatting | bytes 5120 | tf_op jit(solution)/shard_map/reshape | solution.py:235
  0.8 0.0 copy-done.2
  0.8 0.0 copy-done.3
  0.8 0.0 copy-start
  0.8 1.1 %copy-done = bf16[20,16,2,640]{3,2,1,0:T(2,128)(2,1)S(1)} copy-done((bf16[20,16,2,640]{3,2,1,0:T(2,128)(2,1)S(1)}, bf16[20,16,2,640]{3,2,1,0:T(2,128)(2,1)}, u32[]{:S(2)}) %copy-start) | copy-done | bytes 819224
  1.9 0.0 copy-start.1
  1.9 1.1 %copy-done.1 = bf16[20,32,640]{2,1,0:T(8,128)(2,1)S(1)} copy-done((bf16[20,32,640]{2,1,0:T(8,128)(2,1)S(1)}, bf16[20,32,640]{2,1,0:T(8,128)(2,1)}, u32[]{:S(2)}) %copy-start.1) | copy-done | bytes 819224
  3.1 14.1 %shard_map.46 = bf16[16,6144]{1,0:T(8,128)(2,1)S(1)} custom-call(s32[640]{0:T(1024)S(1)} %copy-done.2, s32[32]{0:T(128)S(1)} %copy-done.3, s32[1,640]{1,0:T(1,128)S(1)} %reshape.6.slots_ref, bf16[20,16,2,640]{3,2,1,0:T(2,128)(2,1)S(1)} %copy-done, bf16[20,32,640]{2,1,0:T(8,128)(2,1)S(1)} %copy-done.1), custom_call_target="tpu_custom_call" | custom-call | tf_op jit(solution)/shard_map/pallas_call | solution.py:217
  17.2 0.7 %copy.6 = bf16[16,1,6144]{2,0,1:T(8,128)(2,1)} copy(bf16[16,1,6144]{2,0,1:T(8,128)(2,1)S(1)} %bitcast.1) | data formatting | bytes 393216
Async XLA Ops:
  0.0 0.8 %copy-start.2 = (s32[640]{0:T(1024)S(1)}, s32[640]{0:T(1024)}, u32[]{:S(2)}) copy-start(s32[640]{0:T(1024)} %slots_smem.1) | copy-start | bytes 7684
  0.0 0.8 %copy-start.3 = (s32[32]{0:T(128)S(1)}, s32[32]{0:T(128)}, u32[]{:S(2)}) copy-start(s32[32]{0:T(128)} %cycle_smem.1) | copy-start | bytes 388
  0.8 1.1 %copy-start = (bf16[20,16,2,640]{3,2,1,0:T(2,128)(2,1)S(1)}, bf16[20,16,2,640]{3,2,1,0:T(2,128)(2,1)}, u32[]{:S(2)}) copy-start(bf16[20,16,2,640]{3,2,1,0:T(2,128)(2,1)} %spectra_ref.1) | copy-start | bytes 2457604
  1.9 1.1 %copy-start.1 = (bf16[20,32,640]{2,1,0:T(8,128)(2,1)S(1)}, bf16[20,32,640]{2,1,0:T(8,128)(2,1)}, u32[]{:S(2)}) copy-start(bf16[20,32,640]{2,1,0:T(8,128)(2,1)} %legendre_ref.1) | copy-start | bytes 2457604

commit v2 on v1

--- a/solution.py
+++ b/solution.py
@@ -37,8 +37,9 @@
 
 def kernel(
     waves, levs, blocks,
-    slots_smem, cycle_smem, slots_ref, spectra_ref, legendre_ref, out_ref,
-    spec, leg, send, recv, inner, in_sem, send_sem, recv_sem,
+    slots_ref, cycle_ref, spectra_ref, legendre_ref, out_ref,
+    slots_smem, cycle_smem, slots_vmem, spec, leg, send, recv, inner,
+    small_sem, in_sem, send_sem, recv_sem,
 ):
     slots_dev, pairs_dev, _, degrees = spectra_ref.shape
     rows = legendre_ref.shape[1]
@@ -65,6 +66,13 @@
         )
         return carry
 
+    small = [
+        pltpu.make_async_copy(slots_ref, slots_vmem, small_sem.at[0]),
+        pltpu.make_async_copy(cycle_ref, cycle_smem, small_sem.at[1]),
+        pltpu.make_async_copy(slots_ref, slots_smem, small_sem.at[2]),
+    ]
+    for copy in small:
+        copy.start()
     loads = []
     for g in range(groups):
         part = pl.ds(g * group, group)
@@ -77,9 +85,11 @@
             copy.start()
     lax.fori_loop(1, devices, greet, 0)
 
+    for copy in small:
+        copy.wait()
     points_int = 20 + 4 * cycle_smem[me]
     points = points_int.astype(jnp.float32)
-    slots = slots_ref[...]
+    slots = slots_vmem[...].reshape(1, total)
     slot_rows = 32
     within = iota((slot_rows, total), 1).astype(jnp.float32)
     owner = jnp.floor((within + 0.5) * jnp.float32(1.0 / slots_dev))
@@ -211,28 +221,31 @@
     region = NLON // levs
     blocks = min(region // BLOCK, -(-(20 + 4 * (CYCLES - 1)) // BLOCK))
     width = slots_dev * 2 * pairs_dev
-    smem = pl.BlockSpec(memory_space=pltpu.SMEM)
     vmem = pl.BlockSpec(memory_space=pltpu.VMEM)
-    hbm = pl.BlockSpec(memory_space=pl.ANY)
+    hbm = pl.BlockSpec(memory_space=pltpu.HBM)
     grid = pl.pallas_call(
         functools.partial(kernel, waves, levs, blocks),
-        out_shape=jax.ShapeDtypeStruct((pairs_dev * levs, region), jnp.bfloat16),
-        in_specs=[smem, smem, vmem, hbm, hbm],
+        out_shape=pltpu.VMEM((pairs_dev * levs, region), jnp.bfloat16),
+        in_specs=[hbm] * 4,
         out_specs=vmem,
         scratch_shapes=[
+            pltpu.SMEM((total,), jnp.int32),
+            pltpu.SMEM((waves,), jnp.int32),
+            pltpu.VMEM((total,), jnp.int32),
             pltpu.VMEM((slots_dev, pairs_dev, 2, degrees), jnp.bfloat16),
             pltpu.VMEM((slots_dev, rows, degrees), jnp.bfloat16),
             pltpu.VMEM((rows, 1, width), jnp.float32),
             pltpu.VMEM((levs * waves, 1, width), jnp.float32),
             pltpu.VMEM((BLOCK, 2 * total), jnp.bfloat16),
+            pltpu.SemaphoreType.DMA((3,)),
             pltpu.SemaphoreType.DMA((2, slots_dev * 2 * pairs_dev // 128)),
             pltpu.SemaphoreType.DMA,
             pltpu.SemaphoreType.DMA,
         ],
         compiler_params=pltpu.CompilerParams(
-            collective_id=0, has_side_effects=True, vmem_limit_bytes=48 << 20
+            collective_id=0, has_side_effects=True, vmem_limit_bytes=60 << 20
         ),
-    )(wave_slots, row_cycle, wave_slots.reshape(1, total), spectra, legendre)
+    )(wave_slots, row_cycle, spectra, legendre)
     return grid.reshape(grid.shape[0], 1, region)
 
 

time: 18.1 us -> 13.1 us (0.72)
  local copies, waits for them, and re-layouts: 3.73 us -> 0.68 us
  Pallas kernels: 14.1 us -> 12.3 us
    unnamed x9 -> x1, local copies, waits for them, and re-layouts: 2.97 us -> 0.68 us
    pallas_call x1, Pallas kernels: 14.1 us -> 12.3 us  [shards(): pl.pallas_call(functools.partial(kernel, waves, levs, blocks), out_shape=...]
    reshape x1 -> x0, local copies, waits for them, and re-layouts: 0.76 us -> none  [shards(): wave_slots.reshape(1, total)]
where the time goes in v2:
time: 13.1 us; the launch traced here: 12.9 us
  Pallas kernels  12.3 us (94%)
  local copies, waits for them, and re-layouts  0.68 us (5%)
    pallas_call x1, Pallas kernels, shards(): pl.pallas_call(functools.partial(kernel, waves, levs, blocks), out_shape=...  12.3 us
    unnamed x1, local copies, waits for them, and re-layouts  0.68 us

profile of v2, /device:TPU:0, one launch (start us, length us, event | category | flops | bytes accessed | tf_op | source)
XLA Modules:
  0.0 12.9 jit_solution(6391167101411312189)
XLA Ops:
  0.0 12.3 %shard_map.46 = bf16[16,6144]{1,0:T(8,128)(2,1)S(1)} custom-call(s32[640]{0:T(1024)} %slots_ref.1, s32[32]{0:T(128)} %cycle_ref.1, bf16[20,16,2,640]{3,2,1,0:T(2,128)(2,1)} %spectra_ref.1, bf16[20,32,640]{2,1,0:T(8,128)(2,1)} %legendre_ref.1), custom_call_target="tpu_custom_call" | custom-call | tf_op jit(solution)/shard_map/pallas_call | solution.py:226
  12.3 0.7 %copy.6 = bf16[16,1,6144]{2,0,1:T(8,128)(2,1)} copy(bf16[16,1,6144]{2,0,1:T(8,128)(2,1)S(1)} %bitcast.1) | data formatting | bytes 393216

commit v3 on v2

--- a/solution.py
+++ b/solution.py
@@ -74,8 +74,8 @@
     for copy in small:
         copy.start()
     loads = []
-    for g in range(groups):
-        part = pl.ds(g * group, group)
+    for g in range(1):
+        part = pl.ds(0, slots_dev)
         loads.append((
             pltpu.make_async_copy(spectra_ref.at[part], spec.at[part], in_sem.at[0, g]),
             pltpu.make_async_copy(legendre_ref.at[part], leg.at[part], in_sem.at[1, g]),
@@ -85,8 +85,45 @@
             copy.start()
     lax.fori_loop(1, devices, greet, 0)
 
-    for copy in small:
-        copy.wait()
+    small[2].wait()
+    degree = iota((1, degrees), 1)
+    lane_slot = lax.div(iota((rows, 128), 1), lanes)
+    for g in range(groups):
+        for copy in loads[0] if g == 0 else ():
+            copy.wait()
+        kept = []
+        for k in range(group):
+            r = g * group + k
+            limit = total - slots_smem[me * slots_dev + r]
+            keep = jnp.where(degree < limit, 1.0, 0.0).astype(jnp.bfloat16)
+            kept.append(spec[r].reshape(lanes, degrees) * keep)
+        values = leg[pl.ds(g * group, group)].reshape(group * rows, degrees)
+        product = lax.dot_general(
+            values, jnp.concatenate(kept, axis=0), NT, preferred_element_type=jnp.float32
+        )
+        fourier = product[:rows]
+        for k in range(1, group):
+            fourier = jnp.where(lane_slot == k, product[k * rows : (k + 1) * rows], fourier)
+        fourier = fourier.astype(jnp.bfloat16).astype(jnp.float32)
+        send[:, :, pl.ds(g * 128, 128)] = fourier.reshape(rows, 1, 128)
+
+    slot_here = lev * waves + me
+    pl.semaphore_wait(barrier, devices - 1)
+
+    def deliver(step, carry):
+        wave_to, lev_to = peer(step)
+        pltpu.make_async_remote_copy(
+            src_ref=send.at[wave_to], dst_ref=recv.at[slot_here],
+            send_sem=send_sem, recv_sem=recv_sem,
+            device_id={"wave": wave_to, "lev": lev_to}, device_id_type=pl.DeviceIdType.MESH,
+        ).start()
+        return carry
+
+    lax.fori_loop(1, devices, deliver, 0)
+    recv[slot_here] = send[me]
+
+    small[0].wait()
+    small[1].wait()
     points_int = 20 + 4 * cycle_smem[me]
     points = points_int.astype(jnp.float32)
     slots = slots_vmem[...].reshape(1, total)
@@ -119,42 +156,6 @@
     def table(count, stride, first):
         steps = (iota((count, total), 0) * stride + first).astype(jnp.float32)
         return sincos(order_waves, steps, points, inverse)
-
-    degree = iota((1, degrees), 1)
-    lane_slot = lax.div(iota((rows, 128), 1), lanes)
-    for g in range(groups):
-        for copy in loads[g]:
-            copy.wait()
-        kept = []
-        for k in range(group):
-            r = g * group + k
-            limit = total - slots_smem[me * slots_dev + r]
-            keep = jnp.where(degree < limit, 1.0, 0.0).astype(jnp.bfloat16)
-            kept.append(spec[r].reshape(lanes, degrees) * keep)
-        values = leg[pl.ds(g * group, group)].reshape(group * rows, degrees)
-        product = lax.dot_general(
-            values, jnp.concatenate(kept, axis=0), NT, preferred_element_type=jnp.float32
-        )
-        fourier = product[:rows]
-        for k in range(1, group):
-            fourier = jnp.where(lane_slot == k, product[k * rows : (k + 1) * rows], fourier)
-        fourier = fourier.astype(jnp.bfloat16).astype(jnp.float32)
-        send[:, :, pl.ds(g * 128, 128)] = fourier.reshape(rows, 1, 128)
-
-    slot_here = lev * waves + me
-    pl.semaphore_wait(barrier, devices - 1)
-
-    def deliver(step, carry):
-        wave_to, lev_to = peer(step)
-        pltpu.make_async_remote_copy(
-            src_ref=send.at[wave_to], dst_ref=recv.at[slot_here],
-            send_sem=send_sem, recv_sem=recv_sem,
-            device_id={"wave": wave_to, "lev": lev_to}, device_id_type=pl.DeviceIdType.MESH,
-        ).start()
-        return carry
-
-    lax.fori_loop(1, devices, deliver, 0)
-    recv[slot_here] = send[me]
 
     first = lev * (NLON // levs)
     coarse_cos, coarse_sin = table(BLOCK // FINE, FINE, 0)

time: 13.1 us -> 12.4 us (0.947)
  Pallas kernels: 12.3 us -> 11.6 us
    pallas_call x1, Pallas kernels: 12.3 us -> 11.6 us  [shards(): pl.pallas_call(functools.partial(kernel, waves, levs, blocks), out_shape=...]
where the time goes in v3:
time: 12.4 us; the launch traced here: 12.3 us
  Pallas kernels  11.6 us (94%)
  local copies, waits for them, and re-layouts  0.68 us (5%)
    pallas_call x1, Pallas kernels, shards(): pl.pallas_call(functools.partial(kernel, waves, levs, blocks), out_shape=...  11.6 us
    unnamed x1, local copies, waits for them, and re-layouts  0.68 us

profile of v3, /device:TPU:0, one launch (start us, length us, event | category | flops | bytes accessed | tf_op | source)
XLA Modules:
  0.0 12.3 jit_solution(9949539787168853716)
XLA Ops:
  0.0 11.6 %shard_map.46 = bf16[16,6144]{1,0:T(8,128)(2,1)S(1)} custom-call(s32[640]{0:T(1024)} %slots_ref.1, s32[32]{0:T(128)} %cycle_ref.1, bf16[20,16,2,640]{3,2,1,0:T(2,128)(2,1)} %spectra_ref.1, bf16[20,32,640]{2,1,0:T(8,128)(2,1)} %legendre_ref.1), custom_call_target="tpu_custom_call" | custom-call | tf_op jit(solution)/shard_map/pallas_call | solution.py:227
  11.6 0.7 %copy.6 = bf16[16,1,6144]{2,0,1:T(8,128)(2,1)} copy(bf16[16,1,6144]{2,0,1:T(8,128)(2,1)S(1)} %bitcast.1) | data formatting | bytes 393216

commit v4 on v3

--- a/solution.py
+++ b/solution.py
@@ -74,8 +74,8 @@
     for copy in small:
         copy.start()
     loads = []
-    for g in range(1):
-        part = pl.ds(0, slots_dev)
+    half = groups // 2 * group
+    for g, part in ((0, pl.ds(0, half)), (1, pl.ds(half, slots_dev - half))):
         loads.append((
             pltpu.make_async_copy(spectra_ref.at[part], spec.at[part], in_sem.at[0, g]),
             pltpu.make_async_copy(legendre_ref.at[part], leg.at[part], in_sem.at[1, g]),
@@ -89,7 +89,7 @@
     degree = iota((1, degrees), 1)
     lane_slot = lax.div(iota((rows, 128), 1), lanes)
     for g in range(groups):
-        for copy in loads[0] if g == 0 else ():
+        for copy in loads[0] if g == 0 else loads[1] if g == groups // 2 else ():
             copy.wait()
         kept = []
         for k in range(group):
@@ -192,7 +192,7 @@
     pairs = real.shape[0]
 
     at = iota((pairs, BLOCK), 1) + first
-    step = 7 if blocks % 7 == 0 else 2
+    step = blocks
     for start in range(0, blocks, step):
         turned = []
         for j in range(start, start + step):

time: 12.4 us -> 11.9 us (0.960)
  Pallas kernels: 11.6 us -> 11 us
    pallas_call x1, Pallas kernels: 11.6 us -> 11 us  [shards(): pl.pallas_call(functools.partial(kernel, waves, levs, blocks), out_shape=...]
where the time goes in v4:
time: 11.9 us; the launch traced here: 11.7 us
  Pallas kernels  11 us (92%)
  local copies, waits for them, and re-layouts  0.68 us (6%)
    pallas_call x1, Pallas kernels, shards(): pl.pallas_call(functools.partial(kernel, waves, levs, blocks), out_shape=...  11 us
    unnamed x1, local copies, waits for them, and re-layouts  0.68 us

profile of v4, /device:TPU:0, one launch (start us, length us, event | category | flops | bytes accessed | tf_op | source)
XLA Modules:
  0.0 11.7 jit_solution(10725678613299853169)
XLA Ops:
  0.0 11.0 %shard_map.46 = bf16[16,6144]{1,0:T(8,128)(2,1)S(1)} custom-call(s32[640]{0:T(1024)} %slots_ref.1, s32[32]{0:T(128)} %cycle_ref.1, bf16[20,16,2,640]{3,2,1,0:T(2,128)(2,1)} %spectra_ref.1, bf16[20,32,640]{2,1,0:T(8,128)(2,1)} %legendre_ref.1), custom_call_target="tpu_custom_call" | custom-call | tf_op jit(solution)/shard_map/pallas_call | solution.py:227
  11.1 0.7 %copy.6 = bf16[16,1,6144]{2,0,1:T(8,128)(2,1)} copy(bf16[16,1,6144]{2,0,1:T(8,128)(2,1)S(1)} %bitcast.1) | data formatting | bytes 393216
